TPU v7x, 32 devices: a whole 2x2x4 slice. The times are simulated.
32 devices in a mesh: groups: 2 (over y), seq: 8 (over z, x), batch: 2 (over core).
Axes of the slice: x: 2, y: 2, z: 4, core: 2. Of those that a mesh axis runs over, the one named last changes fastest.
Arguments:
- inputs: bfloat16 [4, 2048, 512], P(('groups', 'batch'), 'seq'), parts along dimension 0, may hold values from -6 to 6
- cotangent: bfloat16 [4, 2048, 512], P(('groups', 'batch'), 'seq'), parts along dimension 0, may hold values from -6 to 6
- kernel_one: bfloat16 [3, 512, 256], P(None, 'seq'), may hold values from -0.15625 to 0.15625
- mix_one: bfloat16 [256, 512], P(None, 'seq'), may hold values from -0.375 to 0.375
- kernel_two: bfloat16 [3, 512, 256], P(None, 'seq'), may hold values from -0.15625 to 0.15625
- mix_two: bfloat16 [256, 512], P(None, 'seq'), may hold values from -0.375 to 0.375
Outputs:
- grad_inputs: bfloat16 [4, 2048, 512], P(('groups', 'batch'), 'seq'), parts along dimension 0
- scaled_first_kernel_gradient: bfloat16 [6, 512, 256], P('groups', ('seq', 'batch')), parts along dimension 0
- grad_kernel_two: bfloat16 [6, 512, 256], P('groups'), parts along dimension 0
There are 2 independent parts, one for each index of `groups`. A program takes and returns all parts, laid end to end along the dimension named above; an argument that names none is the same for every part. Nothing has to cross between parts.
All inputs are finite; a program needn't handle non-finite values.
Results may differ from a plain program's by a relative error of at most 0.014.
Values may be sent and summed in bfloat16 or wider, within the bound.
A program may use at most 64 MiB of HBM per device.

v0:
```python
import math

import jax
import jax.numpy as jnp
from jax import lax
from jax.sharding import PartitionSpec as P

FIRST_SPACING = 38
SECOND_SPACING = 58


def padded_2(cells, sides, width):
    for axis, dim in sides:
        count = lax.axis_size(axis)
        ends = count - 1
        head = lax.slice_in_dim(cells, 0, width, axis=dim)
        tail = lax.slice_in_dim(cells, cells.shape[dim] - width, cells.shape[dim], axis=dim)
        cells = jnp.concatenate(
            [
                lax.ppermute(tail, axis, [(i, (i + 1) % count) for i in range(ends)]),
                cells,
                lax.ppermute(head, axis, [((i + 1) % count, i) for i in range(ends)]),
            ],
            axis=dim,
        )
    return cells


def gelu_exact(v):
    return 0.5 * v * (1.0 + jax.scipy.special.erf(v / math.sqrt(2.0)))


def gelu_slope(v):
    cdf = 0.5 * (1.0 + jax.scipy.special.erf(v / math.sqrt(2.0)))
    return cdf + v * jnp.exp(-0.5 * v * v) / math.sqrt(2.0 * math.pi)


def mat_nn(left, right):
    return jnp.dot(left, right, preferred_element_type=jnp.float32)


def mat_nt(left, right):
    return lax.dot_general(
        left, right, (((1,), (1,)), ((), ())), preferred_element_type=jnp.float32
    )


def mat_tn(left, right):
    return lax.dot_general(
        left, right, (((0,), (0,)), ((), ())), preferred_element_type=jnp.float32
    )


def inner_convolved(before, hidden, after, kernel):
    return mat_nn(before, kernel[0]) + mat_nn(hidden, kernel[1]) + mat_nn(after, kernel[2])


def block_back(stream, hidden, grad_inner, above, below, kernel, grad_out):
    partial_value = jnp.stack(
        [mat_tn(hidden, above), mat_tn(hidden, grad_inner), mat_tn(hidden, below)]
    )
    back = mat_nt(grad_inner, kernel[1]) + mat_nt(above, kernel[0]) + mat_nt(below, kernel[2])
    grad_in = (grad_out.astype(jnp.float32) + back * gelu_slope(stream.astype(jnp.float32))).astype(
        jnp.bfloat16
    )
    return (grad_in, partial_value)


def shards(inputs, cotangent, kernel_one, mix_one, kernel_two, mix_two):
    stream = inputs[0]
    grad_top = cotangent[0]
    length = stream.shape[0]
    first_spacing_offset = FIRST_SPACING
    second_spacing_offset = SECOND_SPACING
    kern_a, mixer_a, kern_b, mixer_b = (
        lax.all_gather(kernel_one, "seq", axis=1, tiled=True),
        lax.all_gather(mix_one, "seq", axis=1, tiled=True),
        lax.all_gather(kernel_two, "seq", axis=1, tiled=True),
        lax.all_gather(mix_two, "seq", axis=1, tiled=True),
    )
    hidden_one = gelu_exact(stream.astype(jnp.float32)).astype(jnp.bfloat16)
    padded = padded_2(hidden_one, (("seq", 0),), first_spacing_offset)
    inner_one = inner_convolved(
        padded[:length], hidden_one, padded[2 * first_spacing_offset :], kern_a
    )
    active_one = gelu_exact(inner_one).astype(jnp.bfloat16)
    middle = (stream.astype(jnp.float32) + mat_nn(active_one, mixer_a)).astype(jnp.bfloat16)
    hidden_two = gelu_exact(middle.astype(jnp.float32)).astype(jnp.bfloat16)
    padded_two = padded_2(hidden_two, (("seq", 0),), second_spacing_offset)
    inner_two = inner_convolved(
        padded_two[:length], hidden_two, padded_two[2 * second_spacing_offset :], kern_b
    )
    grad_inner_two = (mat_nt(grad_top, mixer_b) * gelu_slope(inner_two)).astype(jnp.bfloat16)
    grad_pad_two = padded_2(grad_inner_two, (("seq", 0),), second_spacing_offset)
    grad_mid, partial_two = block_back(
        middle,
        hidden_two,
        grad_inner_two,
        grad_pad_two[2 * second_spacing_offset :],
        grad_pad_two[:length],
        kern_b,
        grad_top,
    )
    factor = float(length * lax.axis_size("seq") * lax.axis_size("batch")) ** (-0.5)
    share_two = lax.psum_scatter(partial_two, ("seq", "batch"), scatter_dimension=1, tiled=True)
    result_two = lax.all_gather(
        (share_two * factor).astype(jnp.bfloat16), ("seq", "batch"), axis=1, tiled=True
    )
    grad_inner_one = (mat_nt(grad_mid, mixer_a) * gelu_slope(inner_one)).astype(jnp.bfloat16)
    padded_gradient_rows = padded_2(grad_inner_one, (("seq", 0),), first_spacing_offset)
    grad_in, partial_one = block_back(
        stream,
        hidden_one,
        grad_inner_one,
        padded_gradient_rows[2 * first_spacing_offset :],
        padded_gradient_rows[:length],
        kern_a,
        grad_mid,
    )
    share_one = lax.psum_scatter(partial_one, ("seq", "batch"), scatter_dimension=1, tiled=True)
    return (grad_in[None], (share_one * factor).astype(jnp.bfloat16), result_two)


def solution(mesh):
    placed = (
        P(("groups", "batch"), "seq", None),
        P(("groups", "batch"), "seq", None),
        P(None, "seq", None),
        P(None, "seq"),
        P(None, "seq", None),
        P(None, "seq"),
    )
    return jax.shard_map(
        shards,
        mesh=mesh,
        in_specs=placed,
        out_specs=(
            P(("groups", "batch"), "seq", None),
            P("groups", ("seq", "batch"), None),
            P("groups", None, None),
        ),
        check_vma=False,
    )
```

profile of v0, /device:TPU:0, one launch (start us, length us, event | category | flops | bytes accessed | tf_op | source)
XLA Modules:
  0.0 294.1 jit_solution(14293805978276323068)
XLA Ops:
  7.2 1.1 fusion.23
  8.4 1.3 collective-permute-start.1
  9.7 5.5 %collective-permute-start = (bf16[38,512]{1,0:T(8,128)(2,1)S(1)}, bf16[38,512]{1,0:T(8,128)(2,1)S(1)}, u32[]{:S(2)}, u32[]{:S(2)}) collective-permute-start(bf16[38,512]{1,0:T(8,128)(2,1)S(1)} %get-tuple-element.5), channel_id=1, source_target_pairs={{0,2},{2,4},{4,6},{6,8},{8,10},{10,12},{12,14},{1,3},{3,5},{5,7},{... | collective-permute-start | bytes 116744 | tf_op jit(solution)/shard_map/ppermute | solution.py:20
  15.2 31.9 %all_gather.15 = bf16[256,512]{0,1:T(8,128)(2,1)S(1)} all-gather(bf16[256,64]{0,1:T(8,128)(2,1)} %param.11), channel_id=1, replica_groups=mesh['groups'=2,'seq'=8,'batch'=2] {'seq'}, dimensions={1}, use_global_device_ids=true | all-gather | bytes 294912 | tf_op jit(solution)/shard_map/all_gather | solution.py:79
  47.1 32.5 %all_gather.16 = bf16[3,512,256]{2,1,0:T(8,128)(2,1)S(1)} all-gather(bf16[3,64,256]{2,1,0:T(8,128)(2,1)} %param.8), channel_id=1, replica_groups=mesh['groups'=2,'seq'=8,'batch'=2] {'seq'}, dimensions={1}, use_global_device_ids=true | all-gather | bytes 884736 | tf_op jit(solution)/shard_map/all_gather | solution.py:76
  79.6 0.3 fusion.49
  79.8 31.7 %all_gather.18 = bf16[3,512,256]{2,1,0:T(8,128)(2,1)S(1)} all-gather(bf16[3,64,256]{2,1,0:T(8,128)(2,1)S(1)} %copy-done.1), channel_id=1, replica_groups=mesh['groups'=2,'seq'=8,'batch'=2] {'seq'}, dimensions={1}, use_global_device_ids=true | all-gather | bytes 884736 | tf_op jit(solution)/shard_map/all_gather | solution.py:78
  111.5 30.8 %all_gather.17 = bf16[256,512]{0,1:T(8,128)(2,1)S(1)} all-gather(bf16[256,64]{0,1:T(8,128)(2,1)S(1)} %copy-done.2), channel_id=1, replica_groups=mesh['groups'=2,'seq'=8,'batch'=2] {'seq'}, dimensions={1}, use_global_device_ids=true | all-gather | bytes 294912 | tf_op jit(solution)/shard_map/all_gather | solution.py:77
  142.3 0.2 fusion.45
  142.6 0.2 fusion.9
  142.8 0.3 multiply_convert_fusion
  143.2 1.4 collective-permute-start.3
  144.7 0.2 fusion.53
  144.9 4.5 %collective-permute-start.2 = (bf16[58,512]{1,0:T(8,128)(2,1)S(1)}, bf16[58,512]{1,0:T(8,128)(2,1)S(1)}, u32[]{:S(2)}, u32[]{:S(2)}) collective-permute-start(bf16[58,512]{1,0:T(8,128)(2,1)S(1)} %get-tuple-element.3), channel_id=1, source_target_pairs={{0,2},{2,4},{4,6},{6,8},{8,10},{10,12},{12,14},{1,3},{3,5},{5,7},{... | collective-permute-start | bytes 178184 | tf_op jit(solution)/shard_map/ppermute | solution.py:20
  149.5 0.1 collective-permute-done.3
  149.5 0.2 fusion.42
  149.8 1.6 collective-permute-done.2
  151.3 0.2 fusion.8
  151.6 0.2 fusion.11
  151.8 4.3 %collective-permute-start.5 = (bf16[58,256]{1,0:T(8,128)(2,1)S(1)}, bf16[58,256]{1,0:T(8,128)(2,1)S(1)}, u32[]{:S(2)}, u32[]{:S(2)}) collective-permute-start(bf16[58,256]{1,0:T(8,128)(2,1)S(1)} %get-tuple-element.9), channel_id=1, source_target_pairs={{0,2},{2,4},{4,6},{6,8},{8,10},{10,12},{12,14},{1,3},{3,5},{5,7},{... | collective-permute-start | bytes 89096 | tf_op jit(solution)/shard_map/ppermute | solution.py:20
  156.1 0.3 convolution_bitcast_fusion.1
  156.4 1.3 collective-permute-start.4
  157.7 0.3 convolution_bitcast_fusion
  158.0 4.2 %collective-permute-done.4 = bf16[58,256]{1,0:T(8,128)(2,1)S(1)} collective-permute-done((bf16[58,256]{1,0:T(8,128)(2,1)S(1)}, bf16[58,256]{1,0:T(8,128)(2,1)S(1)}, u32[]{:S(2)}, u32[]{:S(2)}) %collective-permute-start.4) | collective-permute-done | bytes 29728 | tf_op jit(solution)/shard_map/ppermute | solution.py:22
  162.2 0.3 convolution_bitcast_fusion.2
  162.5 1.2 pad_maximum_fusion.1
  163.8 0.3 fusion.52
  164.1 0.3 convolution_add_fusion.3
  164.3 0.4 copy-done.4
  164.7 0.4 fusion.4
  165.2 0.2 fusion.12
  165.4 4.1 %collective-permute-start.7 = (bf16[38,256]{1,0:T(8,128)(2,1)S(1)}, bf16[38,256]{1,0:T(8,128)(2,1)S(1)}, u32[]{:S(2)}, u32[]{:S(2)}) collective-permute-start(bf16[38,256]{1,0:T(8,128)(2,1)S(1)} %get-tuple-element.7), channel_id=1, source_target_pairs={{0,2},{2,4},{4,6},{6,8},{8,10},{10,12},{12,14},{1,3},{3,5},{5,7},{... | collective-permute-start | bytes 58376 | tf_op jit(solution)/shard_map/ppermute | solution.py:20
  169.5 0.3 convolution_bitcast_fusion.4
  169.8 1.3 collective-permute-start.6
  171.1 0.3 convolution_bitcast_fusion.3
  171.4 4.1 %collective-permute-done.6 = bf16[38,256]{1,0:T(8,128)(2,1)S(1)} collective-permute-done((bf16[38,256]{1,0:T(8,128)(2,1)S(1)}, bf16[38,256]{1,0:T(8,128)(2,1)S(1)}, u32[]{:S(2)}, u32[]{:S(2)}) %collective-permute-start.6) | collective-permute-done | bytes 19488 | tf_op jit(solution)/shard_map/ppermute | solution.py:22
  175.5 0.3 convolution_bitcast_fusion.5
  175.7 1.3 pad_maximum_fusion
  177.1 0.3 fusion.51
  177.3 0.3 convolution_add_fusion.1
  177.6 0.4 copy-done.6
  178.0 1.1 fusion.10
  179.1 43.1 %reduce-scatter.5.cloned.1.call-done = f32[3,32,256]{2,1,0:T(8,128)} async-done(((f32[3,512,256]{2,1,0:T(8,128)}), f32[3,32,256]{2,1,0:T(8,128)}) %reduce-scatter.5.cloned.1.call-update) | async-done | bytes 98320 | tf_op jit(solution)/shard_map/reduce_scatter | solution.py:105
  222.2 0.9 multiply_convert_fusion.3
  223.1 21.5 %all_gather.19 = bf16[3,512,256]{2,1,0:T(8,128)(2,1)S(1)} all-gather(bf16[3,32,256]{2,1,0:T(8,128)(2,1)S(1)} %multiply_convert_fusion.3), channel_id=1, replica_groups=mesh['groups'=2,'seq'=8,'batch'=2] {'seq','batch'}, dimensions={1}, use_global_device_ids=true | all-gather | bytes 835584 | tf_op jit(solution)/shard_map/all_gather | solution.py:106
  244.7 40.2 %reduce-scatter.3.cloned.1.call-done = f32[3,32,256]{2,1,0:T(8,128)} async-done(((f32[3,512,256]{2,1,0:T(8,128)}), f32[3,32,256]{2,1,0:T(8,128)}) %reduce-scatter.3.cloned.1.call-update) | async-done | bytes 98320 | tf_op jit(solution)/shard_map/reduce_scatter | solution.py:120
  284.9 1.5 multiply_convert_fusion.4
  286.4 0.9 copy.10
  (24 shorter events, 0.2 us)
Async XLA Ops:
  7.2 72.4 %copy-start = (bf16[1,256,512]{2,1,0:T(8,128)(2,1)S(1)}, bf16[1,256,512]{2,1,0:T(8,128)(2,1)}, u32[]{:S(2)}) copy-start(bf16[1,256,512]{2,1,0:T(8,128)(2,1)} %param.6) | copy-start | bytes 786436
  7.2 72.7 %copy-start.1 = (bf16[3,64,256]{2,1,0:T(8,128)(2,1)S(1)}, bf16[3,64,256]{2,1,0:T(8,128)(2,1)}, u32[]{:S(2)}) copy-start(bf16[3,64,256]{2,1,0:T(8,128)(2,1)} %param.10) | copy-start | bytes 294916
  7.2 215.1 %reduce-scatter.5.cloned.1.call-start = ((), (), s32[]{:S(2)}) async-start(), calls=%async_computation.3 | async-start | bytes 1671168 | tf_op jit(solution)/shard_map/reduce_scatter | solution.py:105
  8.4 134.0 %collective-permute-start.1 = (bf16[38,512]{1,0:T(8,128)(2,1)S(1)}, bf16[38,512]{1,0:T(8,128)(2,1)S(1)}, u32[]{:S(2)}, u32[]{:S(2)}) collective-permute-start(bf16[38,512]{1,0:T(8,128)(2,1)S(1)} %get-tuple-element.6), channel_id=1, source_target_pairs={{2,0},{4,2},{6,4},{8,6},{10,8},{12,10},{14,12},{3,1},{5,3},{7,5},{... | collective-permute-start | bytes 116744 | tf_op jit(solution)/shard_map/ppermute | solution.py:22
  9.7 101.8 %copy-start.2 = (bf16[256,64]{0,1:T(8,128)(2,1)S(1)}, bf16[256,64]{0,1:T(8,128)(2,1)}, u32[]{:S(2)}) copy-start(bf16[256,64]{0,1:T(8,128)(2,1)} %param.9) | copy-start | bytes 98308
  9.7 132.9 %collective-permute-start = (bf16[38,512]{1,0:T(8,128)(2,1)S(1)}, bf16[38,512]{1,0:T(8,128)(2,1)S(1)}, u32[]{:S(2)}, u32[]{:S(2)}) collective-permute-start(bf16[38,512]{1,0:T(8,128)(2,1)S(1)} %get-tuple-element.5), channel_id=1, source_target_pairs={{0,2},{2,4},{4,6},{6,8},{8,10},{10,12},{12,14},{1,3},{3,5},{5,7},{... | collective-permute-start | bytes 116744 | tf_op jit(solution)/shard_map/ppermute | solution.py:20
  143.2 8.4 %copy-start.3 = (bf16[1,256,512]{2,1,0:T(8,128)(2,1)S(1)}, bf16[1,256,512]{2,1,0:T(8,128)(2,1)}, u32[]{:S(2)}) copy-start(bf16[1,256,512]{2,1,0:T(8,128)(2,1)} %param.7) | copy-start | bytes 786436
  143.2 6.3 %collective-permute-start.3 = (bf16[58,512]{1,0:T(8,128)(2,1)S(1)}, bf16[58,512]{1,0:T(8,128)(2,1)S(1)}, u32[]{:S(2)}, u32[]{:S(2)}) collective-permute-start(bf16[58,512]{1,0:T(8,128)(2,1)S(1)} %get-tuple-element.4), channel_id=1, source_target_pairs={{2,0},{4,2},{6,4},{8,6},{10,8},{12,10},{14,12},{3,1},{5,3},{7,5},{... | collective-permute-start | bytes 178184 | tf_op jit(solution)/shard_map/ppermute | solution.py:22
  144.9 6.4 %collective-permute-start.2 = (bf16[58,512]{1,0:T(8,128)(2,1)S(1)}, bf16[58,512]{1,0:T(8,128)(2,1)S(1)}, u32[]{:S(2)}, u32[]{:S(2)}) collective-permute-start(bf16[58,512]{1,0:T(8,128)(2,1)S(1)} %get-tuple-element.3), channel_id=1, source_target_pairs={{0,2},{2,4},{4,6},{6,8},{8,10},{10,12},{12,14},{1,3},{3,5},{5,7},{... | collective-permute-start | bytes 178184 | tf_op jit(solution)/shard_map/ppermute | solution.py:20
  151.8 5.9 %collective-permute-start.5 = (bf16[58,256]{1,0:T(8,128)(2,1)S(1)}, bf16[58,256]{1,0:T(8,128)(2,1)S(1)}, u32[]{:S(2)}, u32[]{:S(2)}) collective-permute-start(bf16[58,256]{1,0:T(8,128)(2,1)S(1)} %get-tuple-element.9), channel_id=1, source_target_pairs={{0,2},{2,4},{4,6},{6,8},{8,10},{10,12},{12,14},{1,3},{3,5},{5,7},{... | collective-permute-start | bytes 89096 | tf_op jit(solution)/shard_map/ppermute | solution.py:20
  156.4 5.8 %collective-permute-start.4 = (bf16[58,256]{1,0:T(8,128)(2,1)S(1)}, bf16[58,256]{1,0:T(8,128)(2,1)S(1)}, u32[]{:S(2)}, u32[]{:S(2)}) collective-permute-start(bf16[58,256]{1,0:T(8,128)(2,1)S(1)} %get-tuple-element.10), channel_id=1, source_target_pairs={{2,0},{4,2},{6,4},{8,6},{10,8},{12,10},{14,12},{3,1},{5,3},{7,5},{... | collective-permute-start | bytes 89096 | tf_op jit(solution)/shard_map/ppermute | solution.py:22
  163.7 121.1 %reduce-scatter.3.cloned.1.call-start = ((), (), s32[]{:S(2)}) async-start(), calls=%async_computation.2 | async-start | bytes 1671168 | tf_op jit(solution)/shard_map/reduce_scatter | solution.py:120
  163.8 1.0 copy-start.4
  165.1 10.3 %copy-start.5 = (bf16[256,512]{1,0:T(8,128)(2,1)}, bf16[256,512]{1,0:T(8,128)(2,1)S(1)}, u32[]{:S(2)}) copy-start(bf16[256,512]{1,0:T(8,128)(2,1)S(1)} %fusion.4) | copy-start | bytes 786436
  165.4 5.7 %collective-permute-start.7 = (bf16[38,256]{1,0:T(8,128)(2,1)S(1)}, bf16[38,256]{1,0:T(8,128)(2,1)S(1)}, u32[]{:S(2)}, u32[]{:S(2)}) collective-permute-start(bf16[38,256]{1,0:T(8,128)(2,1)S(1)} %get-tuple-element.7), channel_id=1, source_target_pairs={{0,2},{2,4},{4,6},{6,8},{8,10},{10,12},{12,14},{1,3},{3,5},{5,7},{... | collective-permute-start | bytes 58376 | tf_op jit(solution)/shard_map/ppermute | solution.py:20
  169.8 5.7 %collective-permute-start.6 = (bf16[38,256]{1,0:T(8,128)(2,1)S(1)}, bf16[38,256]{1,0:T(8,128)(2,1)S(1)}, u32[]{:S(2)}, u32[]{:S(2)}) collective-permute-start(bf16[38,256]{1,0:T(8,128)(2,1)S(1)} %get-tuple-element.8), channel_id=1, source_target_pairs={{2,0},{4,2},{6,4},{8,6},{10,8},{12,10},{14,12},{3,1},{5,3},{7,5},{... | collective-permute-start | bytes 58376 | tf_op jit(solution)/shard_map/ppermute | solution.py:22
  177.0 1.0 copy-start.6
Sparse Core Ops, SparseCore 0:
  163.9 58.3 reduce-scatter.4
  226.3 58.4 reduce-scatter.2
where the time goes:
time: 295 us; the launch traced here: 294 us
  blocking collectives  148 us (50%)
  waiting for transfers between devices  93.3 us (32%)
  starting transfers between devices  23.8 us (8%)
  between operations  14.4 us (5%)
  matrix products  6.35 us (2%)
  other arithmetic  6.05 us (2%)
    reduce_scatter x1, waiting for transfers between devices, shards(): lax.psum_scatter(partial_two, ('seq', 'batch'), scatter_dimension=1, tile...  43.1 us
    reduce_scatter x1, waiting for transfers between devices, shards(): lax.psum_scatter(partial_one, ('seq', 'batch'), scatter_dimension=1, tile...  40.2 us
    all_gather x1, blocking collectives, shards(): lax.all_gather(kernel_one, 'seq', axis=1, tiled=True)  32.5 us
    all_gather x1, blocking collectives, shards(): lax.all_gather(mix_two, 'seq', axis=1, tiled=True)  31.9 us
    all_gather x1, blocking collectives, shards(): lax.all_gather(kernel_two, 'seq', axis=1, tiled=True)  31.7 us
    all_gather x1, blocking collectives, shards(): lax.all_gather(mix_one, 'seq', axis=1, tiled=True)  30.8 us
    all_gather x1, blocking collectives, shards(): lax.all_gather((share_two * factor).astype(jnp.bfloat16), ('seq', 'batch'...  21.5 us
    ppermute x4, starting transfers between devices, padded_2(): lax.ppermute(tail, axis, [(i, (i + 1) % count) for i in range(ends)])  18.4 us
  transfers between devices with their start and end apart: 10, of which 6 were waited for; matrix products, arithmetic and copies ran while one was open for 2% of the time, Pallas kernels for 0%

commit v1 on v0

--- a/solution.py
+++ b/solution.py
@@ -1,8 +1,11 @@
+import functools
 import math
 
 import jax
 import jax.numpy as jnp
 from jax import lax
+from jax.experimental import pallas as pl
+from jax.experimental.pallas import tpu as pltpu
 from jax.sharding import PartitionSpec as P
 
 FIRST_SPACING = 38
@@ -121,6 +124,460 @@
     return (grad_in[None], (share_one * factor).astype(jnp.bfloat16), result_two)
 
 
+HALO = 256
+MARGIN_MID, MARGIN_TWO, MARGIN_ONE = 192, 128, 64
+TILE = 128
+
+
+def nn(left, right):
+    return jnp.dot(left, right, preferred_element_type=jnp.float32)
+
+
+def nt(left, right):
+    return lax.dot_general(
+        left, right, (((1,), (1,)), ((), ())), preferred_element_type=jnp.float32
+    )
+
+
+def tn(left, right):
+    return lax.dot_general(
+        left, right, (((0,), (0,)), ((), ())), preferred_element_type=jnp.float32
+    )
+
+
+def cdf_of(v):
+    return 0.5 + 0.5 * lax.erf(v * (1.0 / math.sqrt(2.0)))
+
+
+def slope_of(v, cdf):
+    return cdf + v * jnp.exp(-0.5 * v * v) * (1.0 / math.sqrt(2.0 * math.pi))
+
+
+def over_rows(start, stop, tile, body):
+    def step(i, carry):
+        body(pl.multiple_of(start + i * tile, math.gcd(start, tile) if start else tile))
+        return carry
+
+    lax.fori_loop(0, (stop - start) // tile, step, 0)
+
+
+def fused_kernel(
+    n, zs, factor,
+    x_ref, c_ref, k1_ref, m1_ref, k2_ref, m2_ref,
+    gin_ref, first_ref, second_ref,
+    w, xf, cf, h1, s1, a0, a1, a2, u1, v1, x2, h2, s2, u2, du, cat, g1,
+    pb, r1, sm, r2, q, r3, gb,
+    wz_s, wz_r, wx_s, wx_r, wc_s, wc_r, hs, hr, p1s, p1r, p2s, p2r, p3s, p3r,
+    gzs, gzr, gxs, gxr, gcs, gcr,
+):
+    bf, f32 = jnp.bfloat16, jnp.float32
+    s = lax.axis_index("seq")
+    b = lax.axis_index("batch")
+    count = 2 * zs
+    z, xx = s // 2, s % 2
+    xp = s + 1 - 2 * xx
+    rows = k1_ref.shape[1]
+    sub = rows // 2
+
+    def to(seq, batch):
+        return {"seq": seq, "batch": batch}
+
+    def copy(src, dst, send, recv, target):
+        return pltpu.make_async_remote_copy(
+            src_ref=src, dst_ref=dst, send_sem=send, recv_sem=recv,
+            device_id=target, device_id_type=pl.DeviceIdType.MESH,
+        )
+
+    barrier = pltpu.get_barrier_semaphore()
+    away = sorted({1, count - 1} | {2 * r for r in range(1, zs)})
+    for d in away:
+        pl.semaphore_signal(barrier, inc=1, device_id=to((s + d) % count, b), device_id_type=pl.DeviceIdType.MESH)
+    pl.semaphore_signal(barrier, inc=1, device_id=to(s, 1 - b), device_id_type=pl.DeviceIdType.MESH)
+
+    eye = (
+        lax.broadcasted_iota(jnp.int32, (rows, rows), 0) == lax.broadcasted_iota(jnp.int32, (rows, rows), 1)
+    ).astype(f32).astype(bf)
+    for layer, (k_ref, m_ref) in enumerate(((k1_ref, m1_ref), (k2_ref, m2_ref))):
+        for tap in range(3):
+            w[layer, s, tap] = k_ref[tap]
+        w[layer, s, 3] = nt(eye, m_ref[...]).astype(bf)
+    pl.semaphore_wait(barrier, len(away) + 1)
+
+    pending = []
+
+    def launch(c):
+        c.start()
+        pending.append(c)
+        return c
+
+    halos = (
+        (s < count - 1, s > 0, (s + 1) % count, n - HALO, 0, n - MARGIN_TWO, 0, 0),
+        (s > 0, s < count - 1, (s + count - 1) % count, 0, HALO + n, 0, MARGIN_TWO + n, 2),
+    )
+    halo_copies = []
+    for sends, receives, target, xsrc, xdst, csrc, cdst, at in halos:
+        pair = (
+            copy(x_ref.at[pl.ds(xsrc, HALO)], xf.at[pl.ds(xdst, HALO)], hs.at[at], hr.at[at], to(target, b)),
+            copy(c_ref.at[pl.ds(csrc, MARGIN_TWO)], cf.at[pl.ds(cdst, MARGIN_TWO)], hs.at[at + 1], hr.at[at + 1], to(target, b)),
+        )
+        halo_copies.append((sends, receives, pair, xdst, cdst))
+
+    def start_halo(which):
+        for sends, receives, pair, xdst, cdst in halo_copies:
+            @pl.when(sends)
+            def _():
+                pair[which].start()
+
+    def half(layer, seq):
+        return w.at[layer, seq, pl.ds(2 * b, 2)]
+
+    def column(r, other=False):
+        side = 1 - xx if other else xx
+        return ((z + zs - r) % zs) * 2 + side
+
+    wz, wx, wc = {}, {}, {}
+
+    def send_x(layer, r):
+        c = half(layer, column(r))
+        wx[layer, r] = launch(copy(c, c, wx_s.at[layer, r], wx_r.at[layer, r], to(xp, b)))
+
+    def send_core(layer, r, other):
+        c = half(layer, column(r, other))
+        at = r + (zs if other else 0)
+        wc[layer, at] = launch(copy(c, c, wc_s.at[layer, at], wc_r.at[layer, at], to(s, 1 - b)))
+
+    def weights_start(layer):
+        for r in range(1, zs):
+            c = half(layer, s)
+            wz[layer, r] = launch(
+                copy(c, c, wz_s.at[layer, r - 1], wz_r.at[layer, r - 1], to(((z + r) % zs) * 2 + xx, b))
+            )
+        send_x(layer, 0)
+
+    def weights_z(layer):
+        for r in [1, zs - 1] + list(range(2, zs - 1)):
+            wz[layer, r].wait_recv()
+            send_x(layer, r)
+            send_core(layer, r, False)
+
+    def weights_x(layer):
+        for r in [0, 1, zs - 1] + list(range(2, zs - 1)):
+            wx[layer, r].wait_recv()
+            send_core(layer, r, True)
+
+    def weights_core(layer):
+        for at in range(1, 2 * zs):
+            wc[layer, at].wait_recv()
+
+    def tap_of(layer, tap):
+        return w[layer, :, tap].reshape(count * rows, w.shape[-1])
+
+    weights_start(0)
+    start_halo(0)
+    weights_start(1)
+    start_halo(1)
+
+    def own_gelu(t):
+        v = x_ref[pl.ds(t, 16), :]
+        xf[pl.ds(HALO + t, 16), :] = v
+        v = v.astype(f32)
+        cdf = cdf_of(v)
+        h1[pl.ds(HALO + t, 16), :] = (v * cdf).astype(bf)
+        s1[pl.ds(t, 16), :] = slope_of(v, cdf)
+
+    over_rows(0, n, 16, own_gelu)
+    cf[pl.ds(MARGIN_TWO, n), :] = c_ref[...]
+    weights_z(0)
+
+    for sends, receives, pair, xdst, cdst in halo_copies:
+        @pl.when(receives)
+        def _():
+            pair[0].wait_recv()
+
+        @pl.when(jnp.logical_not(receives))
+        def _():
+            xf[pl.ds(xdst, HALO), :] = jnp.zeros((HALO, xf.shape[1]), bf)
+
+    def halo_gelu(t):
+        v = xf[pl.ds(t, 16), :].astype(f32)
+        h1[pl.ds(t, 16), :] = (v * cdf_of(v)).astype(bf)
+
+    over_rows(0, HALO, 16, halo_gelu)
+    weights_x(0)
+    over_rows(HALO + n, 2 * HALO + n, 16, halo_gelu)
+    weights_z(1)
+    weights_core(0)
+
+    def convolve(h, layer, total):
+        def body(t):
+            tile = h[pl.ds(t, TILE), :]
+            a0[pl.ds(t, TILE), :] = nn(tile, tap_of(layer, 0))
+            a1[pl.ds(t, TILE), :] = nn(tile, tap_of(layer, 1))
+            a2[pl.ds(t, TILE), :] = nn(tile, tap_of(layer, 2))
+
+        over_rows(0, total, TILE, body)
+
+    mid = n + 2 * MARGIN_MID
+    two = n + 2 * MARGIN_TWO
+    one = n + 2 * MARGIN_ONE
+
+    convolve(h1, 0, n + 2 * HALO)
+    off = HALO - MARGIN_MID
+    d = FIRST_SPACING
+    for t in range(0, mid, 64):
+        u1[pl.ds(t, 64), :] = (
+            a0[pl.ds(t + off - d, 64), :] + a1[pl.ds(t + off, 64), :] + a2[pl.ds(t + off + d, 64), :]
+        )
+
+    def gelu_u1(t):
+        v = u1[pl.ds(t, 32), :]
+        v1[pl.ds(t, 32), :] = (v * cdf_of(v)).astype(bf)
+
+    over_rows(0, mid, 32, gelu_u1)
+    weights_x(1)
+
+    def mix_body(t):
+        out = xf[pl.ds(t + off, TILE), :].astype(f32) + nt(v1[pl.ds(t, TILE), :], tap_of(0, 3))
+        x2[pl.ds(t, TILE), :] = out.astype(bf)
+
+    over_rows(0, mid, TILE, mix_body)
+
+    def gelu_x2(t):
+        v = x2[pl.ds(t, 16), :].astype(f32)
+        h2[pl.ds(t, 16), :] = (v * cdf_of(v)).astype(bf)
+
+    lead = MARGIN_MID - MARGIN_ONE
+
+    def both_x2(t):
+        v = x2[pl.ds(t, 16), :].astype(f32)
+        cdf = cdf_of(v)
+        h2[pl.ds(t, 16), :] = (v * cdf).astype(bf)
+        s2[pl.ds(t - lead, 16), :] = slope_of(v, cdf)
+
+    over_rows(0, lead, 16, gelu_x2)
+    over_rows(lead, lead + one, 16, both_x2)
+    over_rows(lead + one, mid, 16, gelu_x2)
+
+    @pl.when(s == 0)
+    def _():
+        h2[pl.ds(0, MARGIN_MID), :] = jnp.zeros((MARGIN_MID, h2.shape[1]), bf)
+
+    @pl.when(s == count - 1)
+    def _():
+        h2[pl.ds(MARGIN_MID + n, MARGIN_MID), :] = jnp.zeros((MARGIN_MID, h2.shape[1]), bf)
+
+    weights_core(1)
+    convolve(h2, 1, mid)
+    off2 = MARGIN_MID - MARGIN_TWO
+    d = SECOND_SPACING
+    for t in range(0, two, 64):
+        u2[pl.ds(t, 64), :] = (
+            a0[pl.ds(t + off2 - d, 64), :] + a1[pl.ds(t + off2, 64), :] + a2[pl.ds(t + off2 + d, 64), :]
+        )
+
+    for sends, receives, pair, xdst, cdst in halo_copies:
+        @pl.when(receives)
+        def _():
+            pair[1].wait_recv()
+
+        @pl.when(jnp.logical_not(receives))
+        def _():
+            cf[pl.ds(cdst, MARGIN_TWO), :] = jnp.zeros((MARGIN_TWO, cf.shape[1]), bf)
+
+    def inner_two(t):
+        v = u2[pl.ds(t, 64), :]
+        du[pl.ds(t, 64), :] = nn(cf[pl.ds(t, 64), :], tap_of(1, 3)) * slope_of(v, cdf_of(v))
+
+    over_rows(0, two, 64, inner_two)
+    width = du.shape[1]
+
+    def side_by_side(total, off, d):
+        for t in range(0, total, 64):
+            for k, at in enumerate((off + d, off, off - d)):
+                cat[pl.ds(t, 64), pl.ds(k * width, width)] = du[pl.ds(t + at, 64), :].astype(bf)
+
+    def partial(slot, h, first, offset):
+        for k in range(3):
+            p = tn(h[pl.ds(first, n), :], cat[pl.ds(offset, n), pl.ds(k * width, width)]).astype(bf)
+            for i in range(2 * count):
+                pb[slot, i % 2, (i // 2) % 2, i // 4, k] = p[i * sub : (i + 1) * sub]
+
+    def reduce_core(slot):
+        return launch(copy(pb.at[slot, 1 - b], r1.at[slot], p1s.at[slot], p1r.at[slot], to(s, 1 - b)))
+
+    def reduce_x(slot, c):
+        c.wait_recv()
+
+        def add(side):
+            for i in range(zs):
+                sm[slot, side, i] = (
+                    pb[slot, b, side, i].astype(f32) + r1[slot, side, i].astype(f32)
+                ).astype(bf)
+
+        add(1 - xx)
+        c = launch(copy(sm.at[slot, 1 - xx], r2.at[slot], p2s.at[slot], p2r.at[slot], to(xp, b)))
+        add(xx)
+        return c
+
+    def reduce_z(slot, c):
+        c.wait_recv()
+        for i in range(zs):
+            q[slot, i] = (sm[slot, xx, i].astype(f32) + r2[slot, i].astype(f32)).astype(bf)
+        return [
+            launch(
+                copy(
+                    q.at[slot, (z + r) % zs], r3.at[slot, r - 1], p3s.at[slot, r - 1], p3r.at[slot, r - 1],
+                    to(((z + r) % zs) * 2 + xx, b),
+                )
+            )
+            for r in range(1, zs)
+        ]
+
+    def reduce_end(slot, cs):
+        total = q[slot, z].astype(f32)
+        for r, c in enumerate(cs):
+            c.wait_recv()
+            total += r3[slot, r].astype(f32)
+        return (total * factor).astype(bf)
+
+    side_by_side(one, MARGIN_TWO - MARGIN_ONE, SECOND_SPACING)
+    partial(0, h2, MARGIN_MID, MARGIN_ONE)
+    step_two = reduce_core(0)
+
+    def back_of(t, layer, tile):
+        out = nt(cat[pl.ds(t, tile), pl.ds(0, width)], tap_of(layer, 0))
+        out += nt(cat[pl.ds(t, tile), pl.ds(width, width)], tap_of(layer, 1))
+        return out + nt(cat[pl.ds(t, tile), pl.ds(2 * width, width)], tap_of(layer, 2))
+
+    trim = MARGIN_TWO - MARGIN_ONE
+
+    def grad_two(t):
+        out = cf[pl.ds(t + trim, 64), :].astype(f32) + back_of(t, 1, 64) * s2[pl.ds(t, 64), :]
+        g1[pl.ds(t, 64), :] = out.astype(bf)
+
+    over_rows(0, one, 64, grad_two)
+
+    @pl.when(s == 0)
+    def _():
+        g1[pl.ds(0, MARGIN_ONE), :] = jnp.zeros((MARGIN_ONE, g1.shape[1]), bf)
+
+    @pl.when(s == count - 1)
+    def _():
+        g1[pl.ds(MARGIN_ONE + n, MARGIN_ONE), :] = jnp.zeros((MARGIN_ONE, g1.shape[1]), bf)
+
+    step_two = reduce_x(0, step_two)
+
+    def inner_one(t):
+        v = u1[pl.ds(t + lead, 64), :]
+        du[pl.ds(t, 64), :] = nn(g1[pl.ds(t, 64), :], tap_of(0, 3)) * slope_of(v, cdf_of(v))
+
+    over_rows(0, one, 64, inner_one)
+    side_by_side(n, MARGIN_ONE, FIRST_SPACING)
+    partial(1, h1, HALO, 0)
+    step_one = reduce_core(1)
+    step_two = reduce_z(0, step_two)
+    step_one = reduce_x(1, step_one)
+
+    def grad_one(t):
+        out = g1[pl.ds(t + MARGIN_ONE, 64), :].astype(f32) + back_of(t, 0, 64) * s1[pl.ds(t, 64), :]
+        gin_ref[pl.ds(t, 64), :] = out.astype(bf)
+
+    over_rows(0, n, 64, grad_one)
+
+    gb[b, xx, z] = reduce_end(0, step_two)
+    own = gb.at[b, xx, z]
+    along_z = [
+        launch(copy(own, own, gzs.at[r - 1], gzr.at[r - 1], to(((z + r) % zs) * 2 + xx, b)))
+        for r in range(1, zs)
+    ]
+    step_one = reduce_z(1, step_one)
+    for c in along_z:
+        c.wait_recv()
+    whole = gb.at[b, xx]
+    along_x = launch(copy(whole, whole, gxs, gxr, to(xp, b)))
+    first_ref[...] = reduce_end(1, step_one)
+    along_x.wait_recv()
+    whole = gb.at[b]
+    launch(copy(whole, whole, gcs, gcr, to(s, 1 - b))).wait_recv()
+    for i in range(2 * count):
+        for k in range(3):
+            second_ref[k, pl.ds(i * sub, sub), :] = gb[i % 2, (i // 2) % 2, i // 4, k]
+
+    for c in pending:
+        c.wait_send()
+    for sends, receives, pair, xdst, cdst in halo_copies:
+        @pl.when(sends)
+        def _():
+            pair[0].wait_send()
+            pair[1].wait_send()
+
+
+def fused(count, batch, inputs, cotangent, kernel_one, mix_one, kernel_two, mix_two):
+    n, channels = inputs.shape[1:]
+    _, rows, hid = kernel_one.shape
+    sub = rows // 2
+    zs = count // 2
+    bf, f32 = jnp.bfloat16, jnp.float32
+    mid, two, one, frame = n + 2 * MARGIN_MID, n + 2 * MARGIN_TWO, n + 2 * MARGIN_ONE, n + 2 * HALO
+    vm = pltpu.VMEM
+    dma = pltpu.SemaphoreType.DMA
+    sems = []
+    for shape in ((2, zs - 1), (2, zs), (2, 2 * zs), (4,), (2,), (2,), (2, zs - 1), (zs - 1,)):
+        sems += [dma(shape), dma(shape)]
+    sems += [dma, dma, dma, dma]
+    grads = (3, sub, hid)
+    spec = pl.BlockSpec(memory_space=pltpu.VMEM)
+    gin, first, second = pl.pallas_call(
+        functools.partial(fused_kernel, n, zs, float(n * count * batch) ** (-0.5)),
+        out_shape=(
+            jax.ShapeDtypeStruct((n, channels), bf),
+            jax.ShapeDtypeStruct(grads, bf),
+            jax.ShapeDtypeStruct((3, channels, hid), bf),
+        ),
+        in_specs=[spec] * 6,
+        out_specs=(spec,) * 3,
+        scratch_shapes=[
+            vm((2, count, 4, rows, hid), bf),
+            vm((frame, channels), bf),
+            vm((two, channels), bf),
+            vm((frame, channels), bf),
+            vm((n, channels), f32),
+            vm((frame, hid), f32),
+            vm((frame, hid), f32),
+            vm((frame, hid), f32),
+            vm((mid, hid), f32),
+            vm((mid, hid), bf),
+            vm((mid, channels), bf),
+            vm((mid, channels), bf),
+            vm((one, channels), f32),
+            vm((two, hid), f32),
+            vm((two, hid), f32),
+            vm((one, 3 * hid), bf),
+            vm((one, channels), bf),
+            vm((2, 2, 2, zs) + grads, bf),
+            vm((2, 2, zs) + grads, bf),
+            vm((2, 2, zs) + grads, bf),
+            vm((2, zs) + grads, bf),
+            vm((2, zs) + grads, bf),
+            vm((2, zs - 1) + grads, bf),
+            vm((2, 2, zs) + grads, bf),
+        ]
+        + sems,
+        compiler_params=pltpu.CompilerParams(
+            collective_id=0, has_side_effects=True, vmem_limit_bytes=52 * 2**20
+        ),
+    )(inputs[0], cotangent[0], kernel_one, mix_one, kernel_two, mix_two)
+    return (gin[None], first, second)
+
+
+def body(count, batch, inputs, *rest):
+    n, rows = inputs.shape[1], rest[1].shape[1]
+    fits = n >= HALO and n % TILE == 0 and rows % 32 == 0
+    if fits and count % 2 == 0 and count >= 6 and batch == 2:
+        return fused(count, batch, inputs, *rest)
+    return shards(inputs, *rest)
+
+
 def solution(mesh):
     placed = (
         P(("groups", "batch"), "seq", None),
@@ -131,7 +588,7 @@
         P(None, "seq"),
     )
     return jax.shard_map(
-        shards,
+        functools.partial(body, mesh.shape["seq"], mesh.shape["batch"]),
         mesh=mesh,
         in_specs=placed,
         out_specs=(

time: 295 us -> 75 us (0.25)
  blocking collectives: 148 us -> 0 us
  waiting for transfers between devices: 93.3 us -> 0 us
  Pallas kernels: 0 us -> 68.1 us
  starting transfers between devices: 23.8 us -> 0 us
  between operations: 14.4 us -> 0.69 us
  matrix products: 6.35 us -> 0 us
  other arithmetic: 6.05 us -> 0 us
  local copies, waits for them, and re-layouts: 1.79 us -> 5.89 us
    all_gather x5 -> x0, blocking collectives: 148 us -> none  [the longest x1 32.5 us: shards(): lax.all_gather(kernel_one, 'seq', axis=1, tiled=True)]
    reduce_scatter x2 -> x0, waiting for transfers between devices: 83.3 us -> none  [the longest x1 43.1 us: shards(): lax.psum_scatter(partial_two, ('seq', 'batch'), scatter_dimension=1, tile...]
    pallas_call x0 -> x1, Pallas kernels: none -> 68.1 us  [fused(): pl.pallas_call(functools.partial(fused_kernel, n, zs, float(n * count * b...]
    ppermute x8 -> x0, starting transfers between devices: 23.7 us -> none  [the longest x4 18.4 us: padded_2(): lax.ppermute(tail, axis, [(i, (i + 1) % count) for i in range(ends)])]
    ppermute x8 -> x0, waiting for transfers between devices: 9.99 us -> none  [the longest x4 8.39 us: padded_2(): lax.ppermute(head, axis, [((i + 1) % count, i) for i in range(ends)])]
    dot_general x21 -> x0, matrix products: 6.35 us -> none  [the longest x8 3.01 us: mat_nt(): lax.dot_general(left, right, (((1,), (1,)), ((), ())), preferred_element_...]
    unnamed x15 -> x13, local copies, waits for them, and re-layouts: 1.74 us -> 5.89 us
    convert_element_type x3 -> x0, other arithmetic: 3.53 us -> none  [the longest x1 1.52 us: shards(): (share_one * factor).astype(jnp.bfloat16)]
  transfers between devices with their start and end apart: 10 -> 0, of which waited for: 6 -> 0; matrix products, arithmetic and copies ran while one was open for 2% -> 0% of each run, Pallas kernels for 0% -> 0%
where the time goes in v1:
time: 75 us; the launch traced here: 74.7 us
  Pallas kernels  68.1 us (91%)
  local copies, waits for them, and re-layouts  5.89 us (8%)
    pallas_call x1, Pallas kernels, fused(): pl.pallas_call(functools.partial(fused_kernel, n, zs, float(n * count * b...  68.1 us
    unnamed x13, local copies, waits for them, and re-layouts  5.89 us

profile of v1, /device:TPU:0, one launch (start us, length us, event | category | flops | bytes accessed | tf_op | source)
XLA Modules:
  0.0 74.7 jit_solution(16968571087624840576)
XLA Ops:
  0.6 0.0 copy-start.2
  0.6 0.0 copy-start.3
  0.7 0.9 %copy.9.m1_ref = bf16[256,64]{1,0:T(8,128)(2,1)S(1)} copy(bf16[256,64]{0,1:T(8,128)(2,1)} %param.9) | data formatting | bytes 65536 | tf_op args[3]
  1.6 0.9 %copy.10.m2_ref = bf16[256,64]{1,0:T(8,128)(2,1)S(1)} copy(bf16[256,64]{0,1:T(8,128)(2,1)} %param.11) | data formatting | bytes 65536 | tf_op args[5]
  2.4 0.0 copy-done.2
  2.5 0.0 copy-done.3
  2.5 0.0 copy-start
  2.5 0.9 %copy-done = bf16[1,256,512]{2,1,0:T(8,128)(2,1)S(1)} copy-done((bf16[1,256,512]{2,1,0:T(8,128)(2,1)S(1)}, bf16[1,256,512]{2,1,0:T(8,128)(2,1)}, u32[]{:S(2)}) %copy-start) | copy-done | bytes 262168
  3.4 0.0 copy-start.1
  3.4 0.9 %copy-done.1 = bf16[1,256,512]{2,1,0:T(8,128)(2,1)S(1)} copy-done((bf16[1,256,512]{2,1,0:T(8,128)(2,1)S(1)}, bf16[1,256,512]{2,1,0:T(8,128)(2,1)}, u32[]{:S(2)}) %copy-start.1) | copy-done | bytes 262168
  4.4 68.1 %shard_map.85 = (bf16[256,512]{1,0:T(8,128)(2,1)S(1)}, bf16[3,32,256]{2,1,0:T(8,128)(2,1)S(1)}, bf16[3,512,256]{2,1,0:T(8,128)(2,1)S(1)}) custom-call(bf16[256,512]{1,0:T(8,128)(2,1)S(1)} %bitcast.3, bf16[256,512]{1,0:T(8,128)(2,1)S(1)} %bitcast.4, bf16[3,64,256]{2,1,0:T(8,128)(2,1)S(1)} %copy-done.2, bf16[256,64]{1,0:T(8,128)(2,1)S(1)} %copy.9.m1_ref, ...), custom_call_target="tpu_custom_call" | custom-call | tf_op jit(solution)/shard_map/pallas_call | solution.py:530
  72.5 0.7 copy.14
  73.2 0.6 copy.15
  73.8 0.9 %copy.16 = bf16[3,512,256]{2,1,0:T(8,128)(2,1)} copy(bf16[3,512,256]{2,1,0:T(8,128)(2,1)S(1)} %get-tuple-element.14) | data formatting | bytes 1572864
Async XLA Ops:
  0.6 1.8 %copy-start.2 = (bf16[3,64,256]{2,1,0:T(8,128)(2,1)S(1)}, bf16[3,64,256]{2,1,0:T(8,128)(2,1)}, u32[]{:S(2)}) copy-start(bf16[3,64,256]{2,1,0:T(8,128)(2,1)} %k1_ref.1) | copy-start | bytes 294916
  0.6 1.8 %copy-start.3 = (bf16[3,64,256]{2,1,0:T(8,128)(2,1)S(1)}, bf16[3,64,256]{2,1,0:T(8,128)(2,1)}, u32[]{:S(2)}) copy-start(bf16[3,64,256]{2,1,0:T(8,128)(2,1)} %k2_ref.1) | copy-start | bytes 294916
  2.5 1.0 %copy-start = (bf16[1,256,512]{2,1,0:T(8,128)(2,1)S(1)}, bf16[1,256,512]{2,1,0:T(8,128)(2,1)}, u32[]{:S(2)}) copy-start(bf16[1,256,512]{2,1,0:T(8,128)(2,1)} %param.6) | copy-start | bytes 786436
  3.4 0.9 %copy-start.1 = (bf16[1,256,512]{2,1,0:T(8,128)(2,1)S(1)}, bf16[1,256,512]{2,1,0:T(8,128)(2,1)}, u32[]{:S(2)}) copy-start(bf16[1,256,512]{2,1,0:T(8,128)(2,1)} %param.7) | copy-start | bytes 786436

commit v2 on v1

--- a/solution.py
+++ b/solution.py
@@ -124,8 +124,9 @@
     return (grad_in[None], (share_one * factor).astype(jnp.bfloat16), result_two)
 
 
-HALO = 256
-MARGIN_MID, MARGIN_TWO, MARGIN_ONE = 192, 128, 64
+HALO, MARGIN_MID, MARGIN_ONE = 128, 64, 64
+NEAR = 96
+NEAR_TOP = 48
 TILE = 128
 
 
@@ -166,13 +167,14 @@
     x_ref, c_ref, k1_ref, m1_ref, k2_ref, m2_ref,
     gin_ref, first_ref, second_ref,
     w, xf, cf, h1, s1, a0, a1, a2, u1, v1, x2, h2, s2, u2, du, cat, g1,
-    pb, r1, sm, r2, q, r3, gb,
+    pb, r1, sm, r2, q, r3, gb, db, dh,
     wz_s, wz_r, wx_s, wx_r, wc_s, wc_r, hs, hr, p1s, p1r, p2s, p2r, p3s, p3r,
-    gzs, gzr, gxs, gxr, gcs, gcr,
+    gzs, gzr, gxs, gxr, gcs, gcr, wy_s, wy_r, ds, dr,
 ):
     bf, f32 = jnp.bfloat16, jnp.float32
     s = lax.axis_index("seq")
     b = lax.axis_index("batch")
+    g = lax.axis_index("groups")
     count = 2 * zs
     z, xx = s // 2, s % 2
     xp = s + 1 - 2 * xx
@@ -182,6 +184,8 @@
     def to(seq, batch):
         return {"seq": seq, "batch": batch}
 
+    over_y = {"groups": 1 - g}
+
     def copy(src, dst, send, recv, target):
         return pltpu.make_async_remote_copy(
             src_ref=src, dst_ref=dst, send_sem=send, recv_sem=recv,
@@ -193,6 +197,8 @@
     for d in away:
         pl.semaphore_signal(barrier, inc=1, device_id=to((s + d) % count, b), device_id_type=pl.DeviceIdType.MESH)
     pl.semaphore_signal(barrier, inc=1, device_id=to(s, 1 - b), device_id_type=pl.DeviceIdType.MESH)
+
+    pl.semaphore_signal(barrier, inc=1, device_id=over_y, device_id_type=pl.DeviceIdType.MESH)
 
     eye = (
         lax.broadcasted_iota(jnp.int32, (rows, rows), 0) == lax.broadcasted_iota(jnp.int32, (rows, rows), 1)
@@ -201,7 +207,7 @@
         for tap in range(3):
             w[layer, s, tap] = k_ref[tap]
         w[layer, s, 3] = nt(eye, m_ref[...]).astype(bf)
-    pl.semaphore_wait(barrier, len(away) + 1)
+    pl.semaphore_wait(barrier, len(away) + 2)
 
     pending = []
 
@@ -211,14 +217,21 @@
         return c
 
     halos = (
-        (s < count - 1, s > 0, (s + 1) % count, n - HALO, 0, n - MARGIN_TWO, 0, 0),
-        (s > 0, s < count - 1, (s + count - 1) % count, 0, HALO + n, 0, MARGIN_TWO + n, 2),
-    )
+        (s < count - 1, s > 0, (s + 1) % count, 0),
+        (s > 0, s < count - 1, (s + count - 1) % count, 1),
+    )
+
+    def edge(which, height, near):
+        return (n - near, height - near) if which == 0 else (0, height + n)
+
     halo_copies = []
-    for sends, receives, target, xsrc, xdst, csrc, cdst, at in halos:
+    for sends, receives, target, at in halos:
+        xsrc, xdst = edge(at, HALO, NEAR)
+        csrc, cdst = edge(at, MARGIN_ONE, NEAR_TOP)
         pair = (
-            copy(x_ref.at[pl.ds(xsrc, HALO)], xf.at[pl.ds(xdst, HALO)], hs.at[at], hr.at[at], to(target, b)),
-            copy(c_ref.at[pl.ds(csrc, MARGIN_TWO)], cf.at[pl.ds(cdst, MARGIN_TWO)], hs.at[at + 1], hr.at[at + 1], to(target, b)),
+            copy(x_ref.at[pl.ds(xsrc, NEAR)], xf.at[pl.ds(xdst, NEAR)], hs.at[2 * at], hr.at[2 * at], to(target, b)),
+            copy(c_ref.at[pl.ds(csrc, NEAR_TOP)], cf.at[pl.ds(cdst, NEAR_TOP)], hs.at[2 * at + 1], hr.at[2 * at + 1], to(target, b)),
+            copy(db.at[pl.ds(xsrc, NEAR)], dh.at[at], ds.at[at], dr.at[at], to(target, b)),
         )
         halo_copies.append((sends, receives, pair, xdst, cdst))
 
@@ -228,6 +241,9 @@
             def _():
                 pair[which].start()
 
+    def quarter(layer, seq):
+        return w.at[layer, seq, 2 * b + g]
+
     def half(layer, seq):
         return w.at[layer, seq, pl.ds(2 * b, 2)]
 
@@ -235,11 +251,17 @@
         side = 1 - xx if other else xx
         return ((z + zs - r) % zs) * 2 + side
 
-    wz, wx, wc = {}, {}, {}
+    order = [1, zs - 1] + list(range(2, zs - 1))
+    wz, wx, wy, wc = {}, {}, {}, {}
 
     def send_x(layer, r):
-        c = half(layer, column(r))
+        c = quarter(layer, column(r))
         wx[layer, r] = launch(copy(c, c, wx_s.at[layer, r], wx_r.at[layer, r], to(xp, b)))
+
+    def send_y(layer, r, other):
+        c = quarter(layer, column(r, other))
+        at = r + (zs if other else 0)
+        wy[layer, at] = launch(copy(c, c, wy_s.at[layer, at], wy_r.at[layer, at], over_y))
 
     def send_core(layer, r, other):
         c = half(layer, column(r, other))
@@ -248,21 +270,29 @@
 
     def weights_start(layer):
         for r in range(1, zs):
-            c = half(layer, s)
+            c = quarter(layer, s)
             wz[layer, r] = launch(
                 copy(c, c, wz_s.at[layer, r - 1], wz_r.at[layer, r - 1], to(((z + r) % zs) * 2 + xx, b))
             )
         send_x(layer, 0)
 
     def weights_z(layer):
-        for r in [1, zs - 1] + list(range(2, zs - 1)):
+        for r in order:
             wz[layer, r].wait_recv()
             send_x(layer, r)
+            send_y(layer, r, False)
+
+    def weights_x(layer):
+        for r in [0] + order:
+            wx[layer, r].wait_recv()
+            send_y(layer, r, True)
+
+    def weights_y(layer):
+        for r in order:
+            wy[layer, r].wait_recv()
             send_core(layer, r, False)
-
-    def weights_x(layer):
-        for r in [0, 1, zs - 1] + list(range(2, zs - 1)):
-            wx[layer, r].wait_recv()
+        for r in [0] + order:
+            wy[layer, zs + r].wait_recv()
             send_core(layer, r, True)
 
     def weights_core(layer):
@@ -286,8 +316,18 @@
         s1[pl.ds(t, 16), :] = slope_of(v, cdf)
 
     over_rows(0, n, 16, own_gelu)
-    cf[pl.ds(MARGIN_TWO, n), :] = c_ref[...]
+    cf[pl.ds(MARGIN_ONE, n), :] = c_ref[...]
+
+    def blank(ref, first, height):
+        ref[pl.ds(first, height), :] = jnp.zeros((height, ref.shape[1]), ref.dtype)
+
+    blank(xf, 0, HALO - NEAR)
+    blank(xf, HALO + n + NEAR, HALO - NEAR)
+    blank(cf, 0, MARGIN_ONE - NEAR_TOP)
+    blank(cf, MARGIN_ONE + n + NEAR_TOP, MARGIN_ONE - NEAR_TOP)
     weights_z(0)
+    weights_x(0)
+    weights_y(0)
 
     for sends, receives, pair, xdst, cdst in halo_copies:
         @pl.when(receives)
@@ -296,14 +336,13 @@
 
         @pl.when(jnp.logical_not(receives))
         def _():
-            xf[pl.ds(xdst, HALO), :] = jnp.zeros((HALO, xf.shape[1]), bf)
+            blank(xf, xdst, NEAR)
 
     def halo_gelu(t):
         v = xf[pl.ds(t, 16), :].astype(f32)
         h1[pl.ds(t, 16), :] = (v * cdf_of(v)).astype(bf)
 
     over_rows(0, HALO, 16, halo_gelu)
-    weights_x(0)
     over_rows(HALO + n, 2 * HALO + n, 16, halo_gelu)
     weights_z(1)
     weights_core(0)
@@ -318,7 +357,6 @@
         over_rows(0, total, TILE, body)
 
     mid = n + 2 * MARGIN_MID
-    two = n + 2 * MARGIN_TWO
     one = n + 2 * MARGIN_ONE
 
     convolve(h1, 0, n + 2 * HALO)
@@ -336,27 +374,21 @@
     over_rows(0, mid, 32, gelu_u1)
     weights_x(1)
 
+    weights_y(1)
+
     def mix_body(t):
         out = xf[pl.ds(t + off, TILE), :].astype(f32) + nt(v1[pl.ds(t, TILE), :], tap_of(0, 3))
         x2[pl.ds(t, TILE), :] = out.astype(bf)
 
     over_rows(0, mid, TILE, mix_body)
-
-    def gelu_x2(t):
-        v = x2[pl.ds(t, 16), :].astype(f32)
-        h2[pl.ds(t, 16), :] = (v * cdf_of(v)).astype(bf)
-
-    lead = MARGIN_MID - MARGIN_ONE
 
     def both_x2(t):
         v = x2[pl.ds(t, 16), :].astype(f32)
         cdf = cdf_of(v)
         h2[pl.ds(t, 16), :] = (v * cdf).astype(bf)
-        s2[pl.ds(t - lead, 16), :] = slope_of(v, cdf)
-
-    over_rows(0, lead, 16, gelu_x2)
-    over_rows(lead, lead + one, 16, both_x2)
-    over_rows(lead + one, mid, 16, gelu_x2)
+        s2[pl.ds(t, 16), :] = slope_of(v, cdf)
+
+    over_rows(0, mid, 16, both_x2)
 
     @pl.when(s == 0)
     def _():
@@ -368,13 +400,21 @@
 
     weights_core(1)
     convolve(h2, 1, mid)
-    off2 = MARGIN_MID - MARGIN_TWO
+    off2 = MARGIN_MID
     d = SECOND_SPACING
-    for t in range(0, two, 64):
+    for t in range(0, n, 64):
         u2[pl.ds(t, 64), :] = (
             a0[pl.ds(t + off2 - d, 64), :] + a1[pl.ds(t + off2, 64), :] + a2[pl.ds(t + off2 + d, 64), :]
         )
 
+    def inner_two(t):
+        v = u2[pl.ds(t, 64), :]
+        out = nn(cf[pl.ds(t + MARGIN_ONE, 64), :], tap_of(1, 3)) * slope_of(v, cdf_of(v))
+        db[pl.ds(t, 64), :] = out.astype(bf)
+        du[pl.ds(t + HALO, 64), :] = out
+
+    over_rows(0, n, 64, inner_two)
+    start_halo(2)
     for sends, receives, pair, xdst, cdst in halo_copies:
         @pl.when(receives)
         def _():
@@ -382,13 +422,20 @@
 
         @pl.when(jnp.logical_not(receives))
         def _():
-            cf[pl.ds(cdst, MARGIN_TWO), :] = jnp.zeros((MARGIN_TWO, cf.shape[1]), bf)
-
-    def inner_two(t):
-        v = u2[pl.ds(t, 64), :]
-        du[pl.ds(t, 64), :] = nn(cf[pl.ds(t, 64), :], tap_of(1, 3)) * slope_of(v, cdf_of(v))
-
-    over_rows(0, two, 64, inner_two)
+            blank(cf, cdst, NEAR_TOP)
+
+    blank(du, 0, HALO - NEAR)
+    blank(du, HALO + n + NEAR, HALO - NEAR)
+    for at, (sends, receives, pair, xdst, cdst) in enumerate(halo_copies):
+        @pl.when(receives)
+        def _():
+            pair[2].wait_recv()
+            du[pl.ds(xdst, NEAR), :] = dh[at].astype(f32)
+
+        @pl.when(jnp.logical_not(receives))
+        def _():
+            blank(du, xdst, NEAR)
+
     width = du.shape[1]
 
     def side_by_side(total, off, d):
@@ -440,7 +487,7 @@
             total += r3[slot, r].astype(f32)
         return (total * factor).astype(bf)
 
-    side_by_side(one, MARGIN_TWO - MARGIN_ONE, SECOND_SPACING)
+    side_by_side(one, HALO - MARGIN_ONE, SECOND_SPACING)
     partial(0, h2, MARGIN_MID, MARGIN_ONE)
     step_two = reduce_core(0)
 
@@ -449,10 +496,8 @@
         out += nt(cat[pl.ds(t, tile), pl.ds(width, width)], tap_of(layer, 1))
         return out + nt(cat[pl.ds(t, tile), pl.ds(2 * width, width)], tap_of(layer, 2))
 
-    trim = MARGIN_TWO - MARGIN_ONE
-
     def grad_two(t):
-        out = cf[pl.ds(t + trim, 64), :].astype(f32) + back_of(t, 1, 64) * s2[pl.ds(t, 64), :]
+        out = cf[pl.ds(t, 64), :].astype(f32) + back_of(t, 1, 64) * s2[pl.ds(t, 64), :]
         g1[pl.ds(t, 64), :] = out.astype(bf)
 
     over_rows(0, one, 64, grad_two)
@@ -468,7 +513,7 @@
     step_two = reduce_x(0, step_two)
 
     def inner_one(t):
-        v = u1[pl.ds(t + lead, 64), :]
+        v = u1[pl.ds(t, 64), :]
         du[pl.ds(t, 64), :] = nn(g1[pl.ds(t, 64), :], tap_of(0, 3)) * slope_of(v, cdf_of(v))
 
     over_rows(0, one, 64, inner_one)
@@ -510,6 +555,7 @@
         def _():
             pair[0].wait_send()
             pair[1].wait_send()
+            pair[2].wait_send()
 
 
 def fused(count, batch, inputs, cotangent, kernel_one, mix_one, kernel_two, mix_two):
@@ -518,13 +564,14 @@
     sub = rows // 2
     zs = count // 2
     bf, f32 = jnp.bfloat16, jnp.float32
-    mid, two, one, frame = n + 2 * MARGIN_MID, n + 2 * MARGIN_TWO, n + 2 * MARGIN_ONE, n + 2 * HALO
+    mid, one, frame = n + 2 * MARGIN_MID, n + 2 * MARGIN_ONE, n + 2 * HALO
     vm = pltpu.VMEM
     dma = pltpu.SemaphoreType.DMA
     sems = []
     for shape in ((2, zs - 1), (2, zs), (2, 2 * zs), (4,), (2,), (2,), (2, zs - 1), (zs - 1,)):
         sems += [dma(shape), dma(shape)]
     sems += [dma, dma, dma, dma]
+    sems += [dma((2, 2 * zs)), dma((2, 2 * zs)), dma((2,)), dma((2,))]
     grads = (3, sub, hid)
     spec = pl.BlockSpec(memory_space=pltpu.VMEM)
     gin, first, second = pl.pallas_call(
@@ -539,7 +586,7 @@
         scratch_shapes=[
             vm((2, count, 4, rows, hid), bf),
             vm((frame, channels), bf),
-            vm((two, channels), bf),
+            vm((one, channels), bf),
             vm((frame, channels), bf),
             vm((n, channels), f32),
             vm((frame, hid), f32),
@@ -550,8 +597,8 @@
             vm((mid, channels), bf),
             vm((mid, channels), bf),
             vm((one, channels), f32),
-            vm((two, hid), f32),
-            vm((two, hid), f32),
+            vm((n, hid), f32),
+            vm((frame, hid), f32),
             vm((one, 3 * hid), bf),
             vm((one, channels), bf),
             vm((2, 2, 2, zs) + grads, bf),
@@ -561,6 +608,8 @@
             vm((2, zs) + grads, bf),
             vm((2, zs - 1) + grads, bf),
             vm((2, 2, zs) + grads, bf),
+            vm((n, hid), bf),
+            vm((2, NEAR, hid), bf),
         ]
         + sems,
         compiler_params=pltpu.CompilerParams(
@@ -570,10 +619,10 @@
     return (gin[None], first, second)
 
 
-def body(count, batch, inputs, *rest):
+def body(groups, count, batch, inputs, *rest):
     n, rows = inputs.shape[1], rest[1].shape[1]
     fits = n >= HALO and n % TILE == 0 and rows % 32 == 0
-    if fits and count % 2 == 0 and count >= 6 and batch == 2:
+    if fits and count % 2 == 0 and count >= 6 and batch == 2 and groups == 2:
         return fused(count, batch, inputs, *rest)
     return shards(inputs, *rest)
 
@@ -588,7 +637,7 @@
         P(None, "seq"),
     )
     return jax.shard_map(
-        functools.partial(body, mesh.shape["seq"], mesh.shape["batch"]),
+        functools.partial(body, mesh.shape["groups"], mesh.shape["seq"], mesh.shape["batch"]),
         mesh=mesh,
         in_specs=placed,
         out_specs=(

time: 75 us -> 67 us (0.89); the launches traced: 74.7 us -> 65.7 us
  Pallas kernels: 68.1 us -> 59.2 us
    pallas_call x1, Pallas kernels: 68.1 us -> 59.2 us  [fused(): pl.pallas_call(functools.partial(fused_kernel, n, zs, float(n * count * b...]
where the time goes in v2:
time: 67 us; the launch traced here: 65.7 us
  Pallas kernels  59.2 us (88%)
  local copies, waits for them, and re-layouts  5.89 us (9%)
  between operations  0.69 us (1%)
    pallas_call x1, Pallas kernels, fused(): pl.pallas_call(functools.partial(fused_kernel, n, zs, float(n * count * b...  59.2 us
    unnamed x13, local copies, waits for them, and re-layouts  5.89 us

profile of v2, /device:TPU:0, one launch (start us, length us, event | category | flops | bytes accessed | tf_op | source)
XLA Modules:
  0.0 65.7 jit_solution(11230974880244062206)
XLA Ops:
  0.6 0.0 copy-start.2
  0.6 0.0 copy-start.3
  0.7 0.9 %copy.9.m1_ref = bf16[256,64]{1,0:T(8,128)(2,1)S(1)} copy(bf16[256,64]{0,1:T(8,128)(2,1)} %param.9) | data formatting | bytes 65536 | tf_op args[3]
  1.6 0.9 %copy.10.m2_ref = bf16[256,64]{1,0:T(8,128)(2,1)S(1)} copy(bf16[256,64]{0,1:T(8,128)(2,1)} %param.11) | data formatting | bytes 65536 | tf_op args[5]
  2.4 0.0 copy-done.2
  2.5 0.0 copy-done.3
  2.5 0.0 copy-start
  2.5 0.9 %copy-done = bf16[1,256,512]{2,1,0:T(8,128)(2,1)S(1)} copy-done((bf16[1,256,512]{2,1,0:T(8,128)(2,1)S(1)}, bf16[1,256,512]{2,1,0:T(8,128)(2,1)}, u32[]{:S(2)}) %copy-start) | copy-done | bytes 262168
  3.4 0.0 copy-start.1
  3.4 0.9 %copy-done.1 = bf16[1,256,512]{2,1,0:T(8,128)(2,1)S(1)} copy-done((bf16[1,256,512]{2,1,0:T(8,128)(2,1)S(1)}, bf16[1,256,512]{2,1,0:T(8,128)(2,1)}, u32[]{:S(2)}) %copy-start.1) | copy-done | bytes 262168
  4.4 59.2 %shard_map.85 = (bf16[256,512]{1,0:T(8,128)(2,1)S(1)}, bf16[3,32,256]{2,1,0:T(8,128)(2,1)S(1)}, bf16[3,512,256]{2,1,0:T(8,128)(2,1)S(1)}) custom-call(bf16[256,512]{1,0:T(8,128)(2,1)S(1)} %bitcast.3, bf16[256,512]{1,0:T(8,128)(2,1)S(1)} %bitcast.4, bf16[3,64,256]{2,1,0:T(8,128)(2,1)S(1)} %copy-done.2, bf16[256,64]{1,0:T(8,128)(2,1)S(1)} %copy.9.m1_ref, ...), custom_call_target="tpu_custom_call" | custom-call | tf_op jit(solution)/shard_map/pallas_call | solution.py:577
  63.5 0.7 %copy.14 = bf16[1,256,512]{2,1,0:T(8,128)(2,1)} copy(bf16[1,256,512]{2,1,0:T(8,128)(2,1)S(1)} %bitcast.5) | data formatting | bytes 524288
  64.2 0.6 copy.15
  64.9 0.9 %copy.16 = bf16[3,512,256]{2,1,0:T(8,128)(2,1)} copy(bf16[3,512,256]{2,1,0:T(8,128)(2,1)S(1)} %get-tuple-element.14) | data formatting | bytes 1572864
Async XLA Ops:
  0.6 1.8 %copy-start.2 = (bf16[3,64,256]{2,1,0:T(8,128)(2,1)S(1)}, bf16[3,64,256]{2,1,0:T(8,128)(2,1)}, u32[]{:S(2)}) copy-start(bf16[3,64,256]{2,1,0:T(8,128)(2,1)} %k1_ref.1) | copy-start | bytes 294916
  0.6 1.8 %copy-start.3 = (bf16[3,64,256]{2,1,0:T(8,128)(2,1)S(1)}, bf16[3,64,256]{2,1,0:T(8,128)(2,1)}, u32[]{:S(2)}) copy-start(bf16[3,64,256]{2,1,0:T(8,128)(2,1)} %k2_ref.1) | copy-start | bytes 294916
  2.5 1.0 %copy-start = (bf16[1,256,512]{2,1,0:T(8,128)(2,1)S(1)}, bf16[1,256,512]{2,1,0:T(8,128)(2,1)}, u32[]{:S(2)}) copy-start(bf16[1,256,512]{2,1,0:T(8,128)(2,1)} %param.6) | copy-start | bytes 786436
  3.4 0.9 %copy-start.1 = (bf16[1,256,512]{2,1,0:T(8,128)(2,1)S(1)}, bf16[1,256,512]{2,1,0:T(8,128)(2,1)}, u32[]{:S(2)}) copy-start(bf16[1,256,512]{2,1,0:T(8,128)(2,1)} %param.7) | copy-start | bytes 786436

commit v3 on v2

--- a/solution.py
+++ b/solution.py
@@ -169,7 +169,7 @@
     w, xf, cf, h1, s1, a0, a1, a2, u1, v1, x2, h2, s2, u2, du, cat, g1,
     pb, r1, sm, r2, q, r3, gb, db, dh,
     wz_s, wz_r, wx_s, wx_r, wc_s, wc_r, hs, hr, p1s, p1r, p2s, p2r, p3s, p3r,
-    gzs, gzr, gxs, gxr, gcs, gcr, wy_s, wy_r, ds, dr,
+    gzs, gzr, gxs, gxr, gcs, gcr, wy_s, wy_r, ds, dr, ls,
 ):
     bf, f32 = jnp.bfloat16, jnp.float32
     s = lax.axis_index("seq")
@@ -192,6 +192,10 @@
             device_id=target, device_id_type=pl.DeviceIdType.MESH,
         )
 
+    x_own = pltpu.make_async_copy(x_ref, xf.at[pl.ds(HALO, n)], ls.at[0])
+    c_own = pltpu.make_async_copy(c_ref, cf.at[pl.ds(MARGIN_ONE, n)], ls.at[1])
+    x_own.start()
+    c_own.start()
     barrier = pltpu.get_barrier_semaphore()
     away = sorted({1, count - 1} | {2 * r for r in range(1, zs)})
     for d in away:
@@ -304,19 +308,17 @@
 
     weights_start(0)
     start_halo(0)
-    weights_start(1)
     start_halo(1)
 
     def own_gelu(t):
-        v = x_ref[pl.ds(t, 16), :]
-        xf[pl.ds(HALO + t, 16), :] = v
-        v = v.astype(f32)
+        v = xf[pl.ds(HALO + t, 16), :].astype(f32)
         cdf = cdf_of(v)
         h1[pl.ds(HALO + t, 16), :] = (v * cdf).astype(bf)
         s1[pl.ds(t, 16), :] = slope_of(v, cdf)
 
+    x_own.wait()
     over_rows(0, n, 16, own_gelu)
-    cf[pl.ds(MARGIN_ONE, n), :] = c_ref[...]
+    c_own.wait()
 
     def blank(ref, first, height):
         ref[pl.ds(first, height), :] = jnp.zeros((height, ref.shape[1]), ref.dtype)
@@ -326,6 +328,7 @@
     blank(cf, 0, MARGIN_ONE - NEAR_TOP)
     blank(cf, MARGIN_ONE + n + NEAR_TOP, MARGIN_ONE - NEAR_TOP)
     weights_z(0)
+    weights_start(1)
     weights_x(0)
     weights_y(0)
 
@@ -447,7 +450,8 @@
         for k in range(3):
             p = tn(h[pl.ds(first, n), :], cat[pl.ds(offset, n), pl.ds(k * width, width)]).astype(bf)
             for i in range(2 * count):
-                pb[slot, i % 2, (i // 2) % 2, i // 4, k] = p[i * sub : (i + 1) * sub]
+                pb[slot + k, i % 2, (i // 2) % 2, i // 4] = p[i * sub : (i + 1) * sub]
+            yield reduce_core(slot + k)
 
     def reduce_core(slot):
         return launch(copy(pb.at[slot, 1 - b], r1.at[slot], p1s.at[slot], p1r.at[slot], to(s, 1 - b)))
@@ -488,8 +492,7 @@
         return (total * factor).astype(bf)
 
     side_by_side(one, HALO - MARGIN_ONE, SECOND_SPACING)
-    partial(0, h2, MARGIN_MID, MARGIN_ONE)
-    step_two = reduce_core(0)
+    step_two = list(partial(0, h2, MARGIN_MID, MARGIN_ONE))
 
     def back_of(t, layer, tile):
         out = nt(cat[pl.ds(t, tile), pl.ds(0, width)], tap_of(layer, 0))
@@ -510,7 +513,7 @@
     def _():
         g1[pl.ds(MARGIN_ONE + n, MARGIN_ONE), :] = jnp.zeros((MARGIN_ONE, g1.shape[1]), bf)
 
-    step_two = reduce_x(0, step_two)
+    step_two = [reduce_x(k, step_two[k]) for k in range(3)]
 
     def inner_one(t):
         v = u1[pl.ds(t, 64), :]
@@ -518,10 +521,9 @@
 
     over_rows(0, one, 64, inner_one)
     side_by_side(n, MARGIN_ONE, FIRST_SPACING)
-    partial(1, h1, HALO, 0)
-    step_one = reduce_core(1)
-    step_two = reduce_z(0, step_two)
-    step_one = reduce_x(1, step_one)
+    step_one = list(partial(3, h1, HALO, 0))
+    step_two = [reduce_z(k, step_two[k]) for k in range(3)]
+    step_one = [reduce_x(3 + k, step_one[k]) for k in range(3)]
 
     def grad_one(t):
         out = g1[pl.ds(t + MARGIN_ONE, 64), :].astype(f32) + back_of(t, 0, 64) * s1[pl.ds(t, 64), :]
@@ -529,21 +531,32 @@
 
     over_rows(0, n, 64, grad_one)
 
-    gb[b, xx, z] = reduce_end(0, step_two)
+    for k in range(3):
+        gb[b, xx, z, k] = reduce_end(k, step_two[k])
     own = gb.at[b, xx, z]
     along_z = [
         launch(copy(own, own, gzs.at[r - 1], gzr.at[r - 1], to(((z + r) % zs) * 2 + xx, b)))
         for r in range(1, zs)
     ]
-    step_one = reduce_z(1, step_one)
-    for c in along_z:
+
+    def share(r, other, sends, receives, at, target):
+        block = gb.at[b, 1 - xx if other else xx, (z + zs - r) % zs]
+        return launch(copy(block, block, sends.at[at], receives.at[at], target))
+
+    across = {0: share(0, False, gxs, gxr, 0, to(xp, b))}
+    inside = [share(0, False, gcs, gcr, 0, to(s, 1 - b))]
+    step_one = [reduce_z(3 + k, step_one[k]) for k in range(3)]
+    for r in order:
+        along_z[r - 1].wait_recv()
+        across[r] = share(r, False, gxs, gxr, r, to(xp, b))
+        inside.append(share(r, False, gcs, gcr, r, to(s, 1 - b)))
+    for r in [0] + order:
+        across[r].wait_recv()
+        inside.append(share(r, True, gcs, gcr, zs + r, to(s, 1 - b)))
+    for k in range(3):
+        first_ref[k] = reduce_end(3 + k, step_one[k])
+    for c in inside:
         c.wait_recv()
-    whole = gb.at[b, xx]
-    along_x = launch(copy(whole, whole, gxs, gxr, to(xp, b)))
-    first_ref[...] = reduce_end(1, step_one)
-    along_x.wait_recv()
-    whole = gb.at[b]
-    launch(copy(whole, whole, gcs, gcr, to(s, 1 - b))).wait_recv()
     for i in range(2 * count):
         for k in range(3):
             second_ref[k, pl.ds(i * sub, sub), :] = gb[i % 2, (i // 2) % 2, i // 4, k]
@@ -568,10 +581,10 @@
     vm = pltpu.VMEM
     dma = pltpu.SemaphoreType.DMA
     sems = []
-    for shape in ((2, zs - 1), (2, zs), (2, 2 * zs), (4,), (2,), (2,), (2, zs - 1), (zs - 1,)):
+    for shape in ((2, zs - 1), (2, zs), (2, 2 * zs), (4,), (6,), (6,), (6, zs - 1), (zs - 1,)):
         sems += [dma(shape), dma(shape)]
-    sems += [dma, dma, dma, dma]
-    sems += [dma((2, 2 * zs)), dma((2, 2 * zs)), dma((2,)), dma((2,))]
+    sems += [dma((zs,)), dma((zs,)), dma((2 * zs,)), dma((2 * zs,))]
+    sems += [dma((2, 2 * zs)), dma((2, 2 * zs)), dma((2,)), dma((2,)), dma((2,))]
     grads = (3, sub, hid)
     spec = pl.BlockSpec(memory_space=pltpu.VMEM)
     gin, first, second = pl.pallas_call(
@@ -581,7 +594,7 @@
             jax.ShapeDtypeStruct(grads, bf),
             jax.ShapeDtypeStruct((3, channels, hid), bf),
         ),
-        in_specs=[spec] * 6,
+        in_specs=[pl.BlockSpec(memory_space=pl.ANY)] * 2 + [spec] * 4,
         out_specs=(spec,) * 3,
         scratch_shapes=[
             vm((2, count, 4, rows, hid), bf),
@@ -601,12 +614,12 @@
             vm((frame, hid), f32),
             vm((one, 3 * hid), bf),
             vm((one, channels), bf),
-            vm((2, 2, 2, zs) + grads, bf),
-            vm((2, 2, zs) + grads, bf),
-            vm((2, 2, zs) + grads, bf),
-            vm((2, zs) + grads, bf),
-            vm((2, zs) + grads, bf),
-            vm((2, zs - 1) + grads, bf),
+            vm((6, 2, 2, zs) + grads[1:], bf),
+            vm((6, 2, zs) + grads[1:], bf),
+            vm((6, 2, zs) + grads[1:], bf),
+            vm((6, zs) + grads[1:], bf),
+            vm((6, zs) + grads[1:], bf),
+            vm((6, zs - 1) + grads[1:], bf),
             vm((2, 2, zs) + grads, bf),
             vm((n, hid), bf),
             vm((2, NEAR, hid), bf),

time: 67 us -> 65.2 us (0.973); the launches traced: 65.7 us -> 64.6 us
  Pallas kernels: 59.2 us -> 58.1 us
    pallas_call x1, Pallas kernels: 59.2 us -> 58.1 us  [fused(): pl.pallas_call(functools.partial(fused_kernel, n, zs, float(n * count * b...]
where the time goes in v3:
time: 65.2 us; the launch traced here: 64.6 us
  Pallas kernels  58.1 us (89%)
  local copies, waits for them, and re-layouts  5.89 us (9%)
  between operations  0.69 us (1%)
    pallas_call x1, Pallas kernels, fused(): pl.pallas_call(functools.partial(fused_kernel, n, zs, float(n * count * b...  58.1 us
    unnamed x13, local copies, waits for them, and re-layouts  5.89 us

profile of v3, /device:TPU:0, one launch (start us, length us, event | category | flops | bytes accessed | tf_op | source)
XLA Modules:
  0.0 64.6 jit_solution(14796634922071300492)
XLA Ops:
  0.6 0.0 copy-start.2
  0.6 0.0 copy-start.3
  0.7 0.9 %copy.9.m1_ref = bf16[256,64]{1,0:T(8,128)(2,1)S(1)} copy(bf16[256,64]{0,1:T(8,128)(2,1)} %param.9) | data formatting | bytes 65536 | tf_op args[3]
  1.6 0.9 %copy.10.m2_ref = bf16[256,64]{1,0:T(8,128)(2,1)S(1)} copy(bf16[256,64]{0,1:T(8,128)(2,1)} %param.11) | data formatting | bytes 65536 | tf_op args[5]
  2.4 0.0 copy-done.2
  2.5 0.0 copy-done.3
  2.5 0.0 copy-start
  2.5 0.9 %copy-done = bf16[1,256,512]{2,1,0:T(8,128)(2,1)S(1)} copy-done((bf16[1,256,512]{2,1,0:T(8,128)(2,1)S(1)}, bf16[1,256,512]{2,1,0:T(8,128)(2,1)}, u32[]{:S(2)}) %copy-start) | copy-done | bytes 262168
  3.4 0.0 copy-start.1
  3.4 0.9 %copy-done.1 = bf16[1,256,512]{2,1,0:T(8,128)(2,1)S(1)} copy-done((bf16[1,256,512]{2,1,0:T(8,128)(2,1)S(1)}, bf16[1,256,512]{2,1,0:T(8,128)(2,1)}, u32[]{:S(2)}) %copy-start.1) | copy-done | bytes 262168
  4.4 58.1 %shard_map.85 = (bf16[256,512]{1,0:T(8,128)(2,1)S(1)}, bf16[3,32,256]{2,1,0:T(8,128)(2,1)S(1)}, bf16[3,512,256]{2,1,0:T(8,128)(2,1)S(1)}) custom-call(bf16[256,512]{1,0:T(8,128)(2,1)S(1)} %bitcast.3, bf16[256,512]{1,0:T(8,128)(2,1)S(1)} %bitcast.4, bf16[3,64,256]{2,1,0:T(8,128)(2,1)S(1)} %copy-done.2, bf16[256,64]{1,0:T(8,128)(2,1)S(1)} %copy.9.m1_ref, ...), custom_call_target="tpu_custom_call" | custom-call | tf_op jit(solution)/shard_map/pallas_call | solution.py:590
  62.4 0.7 %copy.14 = bf16[1,256,512]{2,1,0:T(8,128)(2,1)} copy(bf16[1,256,512]{2,1,0:T(8,128)(2,1)S(1)} %bitcast.5) | data formatting | bytes 524288
  63.1 0.6 copy.15
  63.8 0.9 %copy.16 = bf16[3,512,256]{2,1,0:T(8,128)(2,1)} copy(bf16[3,512,256]{2,1,0:T(8,128)(2,1)S(1)} %get-tuple-element.14) | data formatting | bytes 1572864
Async XLA Ops:
  0.6 1.8 %copy-start.2 = (bf16[3,64,256]{2,1,0:T(8,128)(2,1)S(1)}, bf16[3,64,256]{2,1,0:T(8,128)(2,1)}, u32[]{:S(2)}) copy-start(bf16[3,64,256]{2,1,0:T(8,128)(2,1)} %k1_ref.1) | copy-start | bytes 294916
  0.6 1.8 %copy-start.3 = (bf16[3,64,256]{2,1,0:T(8,128)(2,1)S(1)}, bf16[3,64,256]{2,1,0:T(8,128)(2,1)}, u32[]{:S(2)}) copy-start(bf16[3,64,256]{2,1,0:T(8,128)(2,1)} %k2_ref.1) | copy-start | bytes 294916
  2.5 1.0 %copy-start = (bf16[1,256,512]{2,1,0:T(8,128)(2,1)S(1)}, bf16[1,256,512]{2,1,0:T(8,128)(2,1)}, u32[]{:S(2)}) copy-start(bf16[1,256,512]{2,1,0:T(8,128)(2,1)} %param.6) | copy-start | bytes 786436
  3.4 0.9 %copy-start.1 = (bf16[1,256,512]{2,1,0:T(8,128)(2,1)S(1)}, bf16[1,256,512]{2,1,0:T(8,128)(2,1)}, u32[]{:S(2)}) copy-start(bf16[1,256,512]{2,1,0:T(8,128)(2,1)} %param.7) | copy-start | bytes 786436
